TPU v7x, 32 devices: a whole 2x2x4 slice. The times are simulated.
32 devices in a mesh: groups: 2 (over x), blk: 16 (over z, y, core).
Axes of the slice: x: 2, y: 2, z: 4, core: 2. Of those that a mesh axis runs over, the one named last changes fastest.
Arguments:
- queries: bfloat16 [32, 8192], P(('groups', 'blk')), parts along dimension 0, may hold values from -13 to 13
- cache_keys: bfloat16 [8192, 1024], P(('groups', 'blk')), parts along dimension 0, may hold values from -10 to 10
- cache_values: bfloat16 [8192, 1024], P(('groups', 'blk')), parts along dimension 0, may hold values from -5 to 5
- lengths: int32 [32], P(('groups', 'blk')), parts along dimension 0, may hold values from 1 to 256, as said below
- stretch_start: int32 [2], P('groups'), parts along dimension 0, may hold values from 2048 to 4080
- residual: float32 [32, 8192], P(('groups', 'blk')), parts along dimension 0, may hold values from -40 to 40
- out_weight: bfloat16 [8192, 8192], P('blk'), may hold values from -0.0625 to 0.0625
- norm_gain: float32 [8192], replicated, may hold values from 0.25 to 1.75
- gate_weight: bfloat16 [8192, 16384], P(None, 'blk'), may hold values from -0.0625 to 0.0625
- up_weight: bfloat16 [8192, 16384], P(None, 'blk'), may hold values from -0.0625 to 0.0625
- down_weight: bfloat16 [16384, 8192], P('blk'), may hold values from -0.046875 to 0.046875
Outputs:
- layer_out: float32 [32, 8192], P(('groups', 'blk')), parts along dimension 0
There are 2 independent parts, one for each index of `groups`. A program takes and returns all parts, laid end to end along the dimension named above; an argument that names none is the same for every part. Nothing has to cross between parts.
Inputs may be any that keep to these rules, and one draw needn't show every extreme that they name: `lengths`: each shard holds 1 to 256 live slots, and some shard is full.
All inputs are finite; a program needn't handle non-finite values.
Results may differ from a plain program's by a relative error of at most 0.0025.
Values may be sent and summed in bfloat16 or wider, within the bound.
A program may use at most 128 MiB of HBM per device.

v0:
```python
import jax
import jax.numpy as jnp
from jax import lax
from jax.sharding import PartitionSpec as P

QUERY_HEADS = 64
KV_HEADS = 8
HEAD_DIM = 128


NEG_FLOOR = -1e30
EPSILON = 1e-05


def body(
    queries,
    cache_keys,
    cache_values,
    lengths,
    stretch_start,
    residual,
    out_weight,
    norm_gain,
    gate_weight,
    up_weight,
    down_weight,
):
    group_size = QUERY_HEADS // KV_HEADS
    score_scale = HEAD_DIM ** (-0.5)
    span = group_size * HEAD_DIM
    all_queries = lax.all_gather(queries, "blk", axis=0, tiled=True)
    row_count = all_queries.shape[0]
    shard_len = cache_keys.shape[0]
    device = lax.axis_index("blk")
    slot_index = jnp.arange(shard_len, dtype=jnp.int32)
    position = device * shard_len + slot_index
    row_position = stretch_start[0] + jnp.arange(row_count, dtype=jnp.int32)
    visible = (slot_index[None, :] < lengths[0]) & (position[None, :] <= row_position[:, None])
    masked = visible[:, None, :]

    def head_step(head_index, state_in):
        numer_all, denom_all, peak_all = state_in
        q_block = lax.dynamic_slice_in_dim(all_queries, head_index * span, span, 1).reshape(
            row_count, group_size, HEAD_DIM
        )
        k_block = lax.dynamic_slice_in_dim(cache_keys, head_index * HEAD_DIM, HEAD_DIM, 1)
        v_block = lax.dynamic_slice_in_dim(cache_values, head_index * HEAD_DIM, HEAD_DIM, 1)
        scores = (
            jnp.einsum("rgd,kd->rgk", q_block, k_block, preferred_element_type=jnp.float32)
            * score_scale
        )
        local_max = jnp.max(jnp.where(masked, scores, NEG_FLOOR), axis=-1)
        weights = jnp.where(masked, jnp.exp(scores - local_max[:, :, None]), 0.0).astype(
            jnp.bfloat16
        )
        partial_out = jnp.einsum(
            "rgk,kd->rgd", weights, v_block, preferred_element_type=jnp.float32
        )
        partial_den = jnp.sum(weights, axis=-1, dtype=jnp.float32)
        numer_all = lax.dynamic_update_slice_in_dim(
            numer_all, partial_out.reshape(row_count, span), head_index * span, 1
        )
        denom_all = lax.dynamic_update_slice_in_dim(
            denom_all, partial_den, head_index * group_size, 1
        )
        peak_all = lax.dynamic_update_slice_in_dim(peak_all, local_max, head_index * group_size, 1)
        return (numer_all, denom_all, peak_all)

    start_state = (
        jnp.zeros((row_count, QUERY_HEADS * HEAD_DIM), jnp.float32),
        jnp.zeros((row_count, QUERY_HEADS), jnp.float32),
        jnp.zeros((row_count, QUERY_HEADS), jnp.float32),
    )
    numer_all, denom_all, peak_all = lax.fori_loop(0, KV_HEADS, head_step, start_state)
    global_max = lax.pmax(peak_all.astype(jnp.bfloat16), "blk").astype(peak_all.dtype)
    factor = jnp.exp(peak_all - global_max)
    scaled = (numer_all.reshape(row_count, QUERY_HEADS, HEAD_DIM) * factor[:, :, None]).reshape(
        row_count, QUERY_HEADS * HEAD_DIM
    )
    scaled_den = denom_all * factor
    numerator = lax.psum_scatter(scaled, "blk", scatter_dimension=1, tiled=True)
    denominator = lax.psum(scaled_den, "blk")
    col_count = numerator.shape[1]
    head_of = (device * col_count + jnp.arange(col_count, dtype=jnp.int32)) // HEAD_DIM
    head_pick = (jnp.arange(QUERY_HEADS, dtype=jnp.int32)[:, None] == head_of[None, :]).astype(
        jnp.float32
    )
    den_cols = jnp.dot(denominator, head_pick, precision=lax.Precision.HIGHEST)
    attn_cols = (numerator / den_cols).astype(jnp.bfloat16)
    picked = attn_cols
    attn_out = lax.psum_scatter(
        jnp.dot(picked, out_weight, preferred_element_type=jnp.float32),
        "blk",
        scatter_dimension=0,
        tiled=True,
    )
    mixed = residual + attn_out
    normed = (
        mixed * lax.rsqrt(jnp.mean(mixed * mixed, axis=-1, keepdims=True) + EPSILON) * norm_gain
    ).astype(jnp.bfloat16)
    row_piece = lax.all_gather(normed, "blk", axis=0, tiled=True)
    gate_term = jnp.dot(row_piece, gate_weight, preferred_element_type=jnp.float32)
    up_term = jnp.dot(row_piece, up_weight, preferred_element_type=jnp.float32)
    hidden_act = (jax.nn.silu(gate_term) * up_term).astype(jnp.bfloat16)
    picked = hidden_act
    ffn_out = lax.psum_scatter(
        jnp.dot(picked, down_weight, preferred_element_type=jnp.float32),
        "blk",
        scatter_dimension=0,
        tiled=True,
    )
    return mixed + ffn_out


def solution(mesh):
    in_specs = (
        P(("groups", "blk"), None),
        P(("groups", "blk"), None),
        P(("groups", "blk"), None),
        P(("groups", "blk")),
        P("groups"),
        P(("groups", "blk"), None),
        P("blk", None),
        P(),
        P(None, "blk"),
        P(None, "blk"),
        P("blk", None),
    )
    out_specs = P(("groups", "blk"), None)
    return jax.shard_map(body, mesh=mesh, in_specs=in_specs, out_specs=out_specs, check_vma=False)
```

profile of v0, /device:TPU:1, one launch (start us, length us, event | category | flops | bytes accessed | tf_op | source)
XLA Modules:
  0.0 380.7 jit_solution(13834208588220643452)
XLA Ops:
  6.5 24.8 %all-gather = bf16[16,1,8192]{2,1,0:T(2,128)(2,1)S(1)} all-gather(bf16[1,1,8192]{2,1,0:T(2,128)(2,1)} %bitcast.64), channel_id=1, replica_groups=mesh['groups'=2,'blk'=16] {'blk'}, dimensions={0}, use_global_device_ids=true | all-gather | bytes 278528 | tf_op jit(solution)/shard_map/all_gather | solution.py:31
  33.1 24.0 %while.18 = (s32[]{:T(128)}, f32[16,8192]{1,0:T(8,128)S(1)}, f32[16,64]{1,0:T(8,128)S(1)}, f32[16,64]{1,0:T(8,128)S(1)}, bf16[16,8192]{1,0:T(8,128)(2,1)S(1)}, /...) while((s32[]{:T(128)}, f32[16,8192]{1,0:T(8,128)S(1)}, ...), condition=%wide.region_3.4_spmd.clone, body=%wide.region_0.3_spmd.clone.sunk | while | flops 17145608 | bytes 906879 | solution.py:74
  33.2 1.1 select_reduce_fusion.2
  34.3 1.1 fusion.45
  36.1 1.1 select_reduce_fusion.2
  37.2 1.1 fusion.45
  39.2 1.1 select_reduce_fusion.2
  40.2 1.1 fusion.45
  42.2 1.1 select_reduce_fusion.2
  43.2 1.1 fusion.45
  45.2 1.1 select_reduce_fusion.2
  46.3 1.1 fusion.45
  48.2 1.1 select_reduce_fusion.2
  49.3 1.1 fusion.45
  51.2 1.1 select_reduce_fusion.2
  52.3 1.1 fusion.45
  54.2 1.1 select_reduce_fusion.2
  55.3 1.1 fusion.45
  57.1 29.0 %pmax.7 = bf16[16,64]{1,0:T(8,128)(2,1)S(1)} all-reduce(bf16[16,64]{1,0:T(8,128)(2,1)S(1)} %convert_element_type.30), channel_id=1, replica_groups=mesh['groups'=2,'blk'=16] {'blk'}, use_global_device_ids=true, to_apply=%region_4.5 | all-reduce | flops 1024 | bytes 4096 | tf_op jit(solution)/shard_map/pmax | solution.py:75
  86.3 1.1 bitcast_multiply_fusion
  87.6 30.3 %psum.7 = f32[16,64]{1,0:T(8,128)S(1)} all-reduce(f32[16,64]{1,0:T(8,128)S(1)} %get-tuple-element.196), channel_id=1, replica_groups=mesh['groups'=2,'blk'=16] {'blk'}, use_global_device_ids=true, to_apply=%region_6.7 | all-reduce | flops 1024 | bytes 8192 | tf_op jit(solution)/shard_map/psum | solution.py:82
  117.9 21.2 %reduce-scatter.2.cloned.1.call-done = f32[16,512]{1,0:T(8,128)} async-done(((f32[16,8192]{1,0:T(8,128)}), f32[16,512]{1,0:T(8,128)}) %reduce-scatter.2.cloned.1.call-update) | async-done | bytes 32784 | tf_op jit(solution)/shard_map/reduce_scatter | solution.py:81
  139.1 0.9 fusion.11
  140.0 5.4 %fusion.32 = f32[16,8192]{1,0:T(8,128)} fusion(bf16[16,512]{1,0:T(8,128)(2,1)S(1)} %fusion.11, bf16[512,8192]{1,0:T(8,128)(2,1)} %param.19), kind=kOutput, calls=%fused_computation.55 | convolution fusion | flops 134217728 | bytes 8929280 | tf_op jit(solution)/shard_map/dot_general | solution.py:92
  145.5 0.7 dynamic-slice
  146.2 91.0 %all-reduce.5.cloned.1.call-done = f32[16,8192]{1,0:T(8,128)} async-done(((f32[16,8192]{1,0:T(8,128)}), f32[16,8192]{1,0:T(8,128)}) %all-reduce.5.cloned.1.call-update) | async-done | bytes 524304
  237.2 2.3 multiply_reduce_fusion
  240.3 22.2 %all-gather.1 = bf16[16,1,8192]{2,1,0:T(2,128)(2,1)S(1)} all-gather(bf16[1,1,8192]{2,1,0:T(2,128)(2,1)S(1)} %convert_bitcast_fusion), channel_id=1, replica_groups=mesh['groups'=2,'blk'=16] {'blk'}, dimensions={0}, use_global_device_ids=true | all-gather | bytes 278528 | tf_op jit(solution)/shard_map/all_gather | solution.py:101
  262.5 8.0 %fusion.15 = f32[16,1024]{1,0:T(8,128)S(1)} fusion(bf16[8192,1024]{1,0:T(8,128)(2,1)} %param.21, bf16[16,1,8192]{2,1,0:T(2,128)(2,1)S(1)} %all-gather.1), kind=kOutput, calls=%fused_computation.23 | convolution fusion | flops 268435456 | bytes 17104896 | tf_op jit(solution)/shard_map/dot_general | solution.py:102
  270.5 13.7 %fusion.12 = f32[16,8192]{1,0:T(8,128)} fusion(bf16[1024,8192]{1,0:T(8,128)(2,1)} %param.23, bf16[8192,1024]{1,0:T(8,128)(2,1)} %param.22, bf16[16,1,8192]{2,1,0:T(2,128)(2,1)S(1)} %all-gather.1, f32[16,1024]{1,0:T(8,128)S(1)} %fusion.15), kind=kOutput, calls=%fused_computation.20 | convolution fusion | flops 536969216 | bytes 34406400 | tf_op jit(solution)/shard_map/dot_general | solution.py:107
  284.3 87.7 %all-reduce.7.cloned.1.call-done = f32[16,8192]{1,0:T(8,128)} async-done(((f32[16,8192]{1,0:T(8,128)}), f32[16,8192]{1,0:T(8,128)}) %all-reduce.7.cloned.1.call-update) | async-done | bytes 524304
  371.9 2.3 dynamic-slice_add_fusion
  (80 shorter events, 7.2 us)
Async XLA Ops:
  6.5 139.0 %copy-start.2 = (u32[32]{0:T(128)S(1)}, u32[32]{0:T(128)}, u32[]{:S(2)}) copy-start(u32[32]{0:T(128)} %constant.115) | copy-start | bytes 388
  6.5 230.7 %copy-start = (f32[1,8192]{1,0:T(1,128)S(1)}, f32[1,8192]{1,0:T(1,128)}, u32[]{:S(2)}) copy-start(f32[1,8192]{1,0:T(1,128)} %param.18) | copy-start | bytes 98308
  6.5 233.7 %copy-start.1 = (f32[8192]{0:T(1024)S(1)}, f32[8192]{0:T(1024)}, u32[]{:S(2)}) copy-start(f32[8192]{0:T(1024)} %param.20) | copy-start | bytes 98308
  6.5 132.6 %reduce-scatter.2.cloned.1.call-start = ((), (), s32[]{:S(2)}) async-start(), calls=%async_computation.1 | async-start | bytes 557056 | tf_op jit(solution)/shard_map/reduce_scatter | solution.py:81
  87.5 149.7 %all-reduce.5.cloned.1.call-start = ((), (), s32[]{:S(2)}) async-start(), calls=%async_computation.2 | async-start | bytes 1048576
  145.5 226.4 %all-reduce.7.cloned.1.call-start = ((), (), s32[]{:S(2)}) async-start(), calls=%async_computation.3 | async-start | bytes 1048576
Sparse Core Ops, SparseCore 0:
  87.6 51.4 reduce-scatter.1
  145.6 91.5 all-reduce.4
  284.4 87.4 all-reduce.6
where the time goes:
time: 382 us; the launch traced here: 381 us
  waiting for transfers between devices  200 us (52%)
  blocking collectives  106 us (28%)
  matrix products  45.2 us (12%)
  between operations  15.2 us (4%)
  other arithmetic  7.81 us (2%)
  local copies, waits for them, and re-layouts  5.68 us (1%)
    unnamed x5, waiting for transfers between devices  179 us
    psum x1, blocking collectives, body(): denominator = lax.psum(scaled_den, 'blk')  30.3 us
    pmax x1, blocking collectives, body(): lax.pmax(peak_all.astype(jnp.bfloat16), 'blk').astype(peak_all.dtype)  29 us
    all_gather x1, blocking collectives, body(): all_queries = lax.all_gather(queries, 'blk', axis=0, tiled=True)  24.8 us
    all_gather x1, blocking collectives, body(): row_piece = lax.all_gather(normed, 'blk', axis=0, tiled=True)  22.2 us
    reduce_scatter x1, waiting for transfers between devices, body(): numerator = lax.psum_scatter(scaled, 'blk', scatter_dimension=1, tiled=True)  21.2 us
    dot_general x1, matrix products, body(): jnp.dot(picked, down_weight, preferred_element_type=jnp.float32)  13.7 us
    dot_general x8, matrix products, head_step(): jnp.einsum('rgd,kd->rgk', q_block, k_block, preferred_element_type=jnp.fl...  8.7 us
  transfers between devices with their start and end apart: 3, of which 3 were waited for; matrix products, arithmetic and copies ran while one was open for 0% of the time, Pallas kernels for 0%

commit v1 on v0

v1 whole, which is shorter than its diff:
```python
import functools

import jax
import jax.numpy as jnp
from jax import lax
from jax.experimental import pallas as pl
from jax.experimental.pallas import tpu as pltpu
from jax.sharding import PartitionSpec as P

QUERY_HEADS = 64
KV_HEADS = 8
HEAD_DIM = 128
GROUP = QUERY_HEADS // KV_HEADS
WIDTH = QUERY_HEADS * HEAD_DIM
NEG_FLOOR = -1e30
EPSILON = 1e-05
F32 = jnp.float32
BF16 = jnp.bfloat16
MESH = pl.DeviceIdType.MESH


def kernel(
    n, ctx, cols, hpd, chunk,
    len_ref, start_ref, q_ref, res_ref, gain_ref, k_hbm, v_hbm, wo_hbm, wg_hbm, wu_hbm, wd_hbm,
    out_ref,
    k_buf, v_buf, wo_buf, wg_buf, wu_buf, wd_buf,
    q_recv, row_f32, qh, msg, msg_recv, part, proj_recv, norm_row, norm_recv, x_buf, ffn_part,
    ffn_recv, hid_buf,
    load_sem, send_sem, recv_sem,
):
    me = lax.axis_index("blk")
    half = wo_buf.shape[0]

    k_load = pltpu.make_async_copy(k_hbm, k_buf, load_sem.at[0])
    v_load = pltpu.make_async_copy(v_hbm, v_buf, load_sem.at[1])
    wo_load = pltpu.make_async_copy(wo_hbm, wo_buf, load_sem.at[2])
    wg_load = pltpu.make_async_copy(wg_hbm, wg_buf, load_sem.at[3])
    wu_load = pltpu.make_async_copy(wu_hbm, wu_buf, load_sem.at[4])
    wd_load = pltpu.make_async_copy(wd_hbm.at[pl.ds(0, half)], wd_buf, load_sem.at[5])
    wd2_load = pltpu.make_async_copy(wd_hbm.at[pl.ds(half, half)], wo_buf, load_sem.at[6])
    for load in (k_load, v_load, wo_load, wg_load, wu_load, wd_load):
        load.start()

    barrier = pltpu.get_barrier_semaphore()

    def greet(i, c):
        pl.semaphore_signal(
            barrier, inc=1, device_id={"blk": lax.rem(me + i, n)}, device_id_type=MESH
        )
        return c

    lax.fori_loop(1, n, greet, 0)
    pl.semaphore_wait(barrier, n - 1)

    def send(phase, src, dst, to):
        pltpu.make_async_remote_copy(
            src_ref=src,
            dst_ref=dst,
            send_sem=send_sem.at[phase],
            recv_sem=recv_sem.at[phase],
            device_id={"blk": to},
            device_id_type=MESH,
        ).start()

    def await_all(sem, buf):
        view = buf.at[pl.ds(0, n - 1)]
        pltpu.make_async_copy(view, view, sem).wait()

    def send_to_all(phase, src, buf):
        def step(i, c):
            send(phase, src, buf.at[me], lax.rem(me + i, n))
            return c

        lax.fori_loop(1, n, step, 0)

    def scatter(phase, parts, buf):
        def step(i, c):
            to = lax.rem(me + i, n)
            send(phase, parts.at[to], buf.at[me], to)
            return c

        lax.fori_loop(1, n, step, 0)

    send_to_all(0, q_ref, q_recv)
    q_recv[me] = q_ref[...]
    await_all(recv_sem.at[0], q_recv)
    row_f32[...] = q_recv[...].astype(F32)
    for h in range(QUERY_HEADS):
        g, i = divmod(h, GROUP)
        qh[g, i * n : (i + 1) * n, :] = row_f32[:, h, :].astype(BF16)
    k_load.wait()
    v_load.wait()

    slot = lax.broadcasted_iota(jnp.int32, (GROUP * n, ctx), 1)
    row = lax.rem(lax.broadcasted_iota(jnp.int32, (GROUP * n, ctx), 0), n)
    visible = (slot < len_ref[0]) & (me * ctx + slot <= start_ref[0] + row)
    lane = lax.broadcasted_iota(jnp.int32, (n, HEAD_DIM), 1)
    dpg = n // KV_HEADS
    per_head = max(HEAD_DIM // cols, 1)

    def head_step(step, carry):
        g = lax.rem(me // dpg + 1 + step, KV_HEADS)
        at = pl.ds(pl.multiple_of(g * HEAD_DIM, HEAD_DIM), HEAD_DIM)
        scores = lax.dot_general(
            qh[g], k_buf[:, at], (((1,), (1,)), ((), ())), preferred_element_type=F32
        ) * (HEAD_DIM ** -0.5)
        peak = jnp.max(jnp.where(visible, scores, NEG_FLOOR), axis=1, keepdims=True)
        peak = peak.astype(BF16).astype(F32)
        weights = jnp.where(visible, jnp.exp(scores - peak), 0.0).astype(BF16)
        total = jnp.sum(weights.astype(F32), axis=1, keepdims=True)
        numer = jnp.dot(weights, v_buf[:, at], preferred_element_type=F32)
        total_hi = total.astype(BF16).astype(F32)
        total_lo = total - total_hi
        for d in range(dpg):
            to = g * dpg + d
            stats = jnp.zeros((n, HEAD_DIM), F32)
            for i in range(hpd):
                h = d * hpd + i if per_head == 1 else d // per_head
                rows = slice(h * n, (h + 1) * n)
                block = numer[rows, :]
                if per_head > 1:
                    lo = (d % per_head) * cols
                    block = block[:, lo : lo + cols]
                msg[to, :, HEAD_DIM * (i + 1) : HEAD_DIM * (i + 1) + block.shape[1]] = block.astype(BF16)
                stats = jnp.where(lane == i, peak[rows, :], stats)
                stats = jnp.where(lane == hpd + i, total_hi[rows, :], stats)
                stats = jnp.where(lane == 2 * hpd + i, total_lo[rows, :], stats)
            msg[to, :, 0:HEAD_DIM] = stats.astype(BF16)

            @pl.when(to != me)
            def _():
                send(1, msg.at[to], msg_recv.at[me], to)

        return carry

    lax.fori_loop(0, KV_HEADS, head_step, 0)
    msg_recv[me] = msg[me]
    await_all(recv_sem.at[1], msg_recv)

    def top_step(d, top):
        return jnp.maximum(top, msg_recv[d, :, 0:HEAD_DIM].astype(F32))

    top = lax.fori_loop(0, n, top_step, jnp.full((n, HEAD_DIM), NEG_FLOOR, F32))
    piece = min(cols, HEAD_DIM)

    def join_step(d, state):
        stats = msg_recv[d, :, 0:HEAD_DIM].astype(F32)
        factor = jnp.exp(jnp.minimum(stats - top, 0.0))
        joined = []
        for i in range(hpd):
            f = factor[:, i : i + 1]
            den = stats[:, hpd + i : hpd + i + 1] + stats[:, 2 * hpd + i : 2 * hpd + i + 1]
            num = msg_recv[d, :, HEAD_DIM * (i + 1) : HEAD_DIM * (i + 1) + piece].astype(F32)
            joined += [state[2 * i] + f * num, state[2 * i + 1] + f * den]
        return tuple(joined)

    zero = (jnp.zeros((n, piece), F32), jnp.zeros((n, 1), F32)) * hpd
    state = lax.fori_loop(0, n, join_step, zero)
    attn = jnp.concatenate(
        [(state[2 * i] / state[2 * i + 1]).astype(BF16) for i in range(hpd)], axis=1
    )

    wo_load.wait()
    for c in range(WIDTH // chunk):
        p = jnp.dot(attn, wo_buf[:, c * chunk : (c + 1) * chunk], preferred_element_type=F32)
        for s in range(chunk // HEAD_DIM):
            row_f32[:, c * (chunk // HEAD_DIM) + s, :] = p[:, s * HEAD_DIM : (s + 1) * HEAD_DIM]
    wd2_load.start()
    part[...] = row_f32[...].astype(BF16)
    scatter(2, part, proj_recv)
    proj_recv[me] = part[me]
    await_all(recv_sem.at[2], proj_recv)

    def add_rows(buf, base):
        def step(d, acc):
            return acc + buf[d].astype(F32)

        return lax.fori_loop(0, n, step, base)

    mixed = res_ref[...] + add_rows(proj_recv, jnp.zeros((QUERY_HEADS, HEAD_DIM), F32))
    mean = jnp.sum(
        jnp.sum(mixed * mixed, axis=1, keepdims=True), axis=0, keepdims=True
    ) * (1.0 / WIDTH)
    norm_row[...] = (mixed * lax.rsqrt(mean + EPSILON) * gain_ref[...]).astype(BF16)
    send_to_all(3, norm_row, norm_recv)
    norm_recv[me] = norm_row[...]
    out_ref[...] = mixed
    await_all(recv_sem.at[3], norm_recv)
    row_f32[...] = norm_recv[...].astype(F32)
    for h in range(QUERY_HEADS):
        x_buf[:, h * HEAD_DIM : (h + 1) * HEAD_DIM] = row_f32[:, h, :].astype(BF16)

    wg_load.wait()
    wu_load.wait()
    hidden = wg_buf.shape[1]
    tile = min(hidden, 256)

    def hidden_step(j, c):
        at = pl.ds(pl.multiple_of(j * tile, tile), tile)
        gate = jnp.dot(x_buf[...], wg_buf[:, at], preferred_element_type=F32)
        up = jnp.dot(x_buf[...], wu_buf[:, at], preferred_element_type=F32)
        hid_buf[:, at] = (gate / (1.0 + jnp.exp(-gate)) * up).astype(BF16)
        return c

    lax.fori_loop(0, hidden // tile, hidden_step, 0)
    wd_load.wait()
    wd2_load.wait()
    act = hid_buf[...]
    for c in range(WIDTH // chunk):
        at = slice(c * chunk, (c + 1) * chunk)
        p = jnp.dot(act[:, :half], wd_buf[:, at], preferred_element_type=F32) + jnp.dot(
            act[:, half:], wo_buf[:, at], preferred_element_type=F32
        )
        for s in range(chunk // HEAD_DIM):
            row_f32[:, c * (chunk // HEAD_DIM) + s, :] = p[:, s * HEAD_DIM : (s + 1) * HEAD_DIM]
    ffn_part[...] = row_f32[...].astype(BF16)
    scatter(4, ffn_part, ffn_recv)
    ffn_recv[me] = ffn_part[me]
    await_all(recv_sem.at[4], ffn_recv)
    out_ref[...] = out_ref[...] + add_rows(ffn_recv, jnp.zeros((QUERY_HEADS, HEAD_DIM), F32))
    for phase, buf in enumerate((q_recv, msg_recv, proj_recv, norm_recv, ffn_recv)):
        await_all(send_sem.at[phase], buf)


def body(
    n, queries, cache_keys, cache_values, lengths, stretch_start, residual, out_weight, norm_gain,
    gate_weight, up_weight, down_weight,
):
    ctx = cache_keys.shape[0]
    cols = WIDTH // n
    hpd = max(cols // HEAD_DIM, 1)
    chunk = 1024
    block = (QUERY_HEADS, HEAD_DIM)
    vmem = pl.BlockSpec(memory_space=pltpu.VMEM)
    smem = pl.BlockSpec(memory_space=pltpu.SMEM)
    any_ = pl.BlockSpec(memory_space=pl.ANY)
    hidden = gate_weight.shape[1]
    half = out_weight.shape[0]
    rows_of = pltpu.VMEM((n, *block), BF16)
    out = pl.pallas_call(
        functools.partial(kernel, n, ctx, cols, hpd, chunk),
        out_shape=jax.ShapeDtypeStruct(block, F32),
        in_specs=[smem, smem, vmem, vmem, vmem] + [any_] * 6,
        out_specs=vmem,
        scratch_shapes=[
            pltpu.VMEM(cache_keys.shape, BF16),
            pltpu.VMEM(cache_values.shape, BF16),
            pltpu.VMEM(out_weight.shape, BF16),
            pltpu.VMEM(gate_weight.shape, BF16),
            pltpu.VMEM(up_weight.shape, BF16),
            pltpu.VMEM((half, WIDTH), BF16),
            rows_of,
            pltpu.VMEM((n, *block), F32),
            pltpu.VMEM((KV_HEADS, GROUP * n, HEAD_DIM), BF16),
            pltpu.VMEM((n, n, HEAD_DIM * (hpd + 1)), BF16),
            pltpu.VMEM((n, n, HEAD_DIM * (hpd + 1)), BF16),
            rows_of,
            rows_of,
            pltpu.VMEM(block, BF16),
            rows_of,
            pltpu.VMEM((n, WIDTH), BF16),
            rows_of,
            rows_of,
            pltpu.VMEM((n, hidden), BF16),
            pltpu.SemaphoreType.DMA((7,)),
            pltpu.SemaphoreType.DMA((5,)),
            pltpu.SemaphoreType.DMA((5,)),
        ],
        compiler_params=pltpu.CompilerParams(
            collective_id=0, has_side_effects=True, vmem_limit_bytes=60 * 1024 * 1024
        ),
    )(
        lengths, stretch_start, queries.reshape(block), residual.reshape(block),
        norm_gain.reshape(block), cache_keys, cache_values, out_weight, gate_weight, up_weight,
        down_weight,
    )
    return out.reshape(1, WIDTH)


def solution(mesh):
    in_specs = (
        P(("groups", "blk"), None),
        P(("groups", "blk"), None),
        P(("groups", "blk"), None),
        P(("groups", "blk")),
        P("groups"),
        P(("groups", "blk"), None),
        P("blk", None),
        P(),
        P(None, "blk"),
        P(None, "blk"),
        P("blk", None),
    )
    out_specs = P(("groups", "blk"), None)
    return jax.shard_map(
        functools.partial(body, mesh.shape["blk"]),
        mesh=mesh,
        in_specs=in_specs,
        out_specs=out_specs,
        check_vma=False,
    )
```

time: 382 us -> 60.8 us (0.16)
  waiting for transfers between devices: 200 us -> 0 us
  blocking collectives: 106 us -> 0 us
  Pallas kernels: 0 us -> 56.1 us
  matrix products: 45.2 us -> 0 us
  between operations: 15.2 us -> 1.31 us
  other arithmetic: 7.81 us -> 1.45 us
  local copies, waits for them, and re-layouts: 5.68 us -> 1.38 us
    unnamed x5 -> x0, waiting for transfers between devices: 179 us -> none
    pallas_call x0 -> x1, Pallas kernels: none -> 56.1 us  [body(): pl.pallas_call(functools.partial(kernel, n, ctx, cols, hpd, chunk), out_s...]
    all_gather x2 -> x0, blocking collectives: 47 us -> none  [the longest x1 24.8 us: body(): all_queries = lax.all_gather(queries, 'blk', axis=0, tiled=True)]
    dot_general x20 -> x0, matrix products: 45.2 us -> none  [the longest x1 13.7 us: body(): jnp.dot(picked, down_weight, preferred_element_type=jnp.float32)]
    psum x1 -> x0, blocking collectives: 30.3 us -> none  [body(): denominator = lax.psum(scaled_den, 'blk')]
    pmax x1 -> x0, blocking collectives: 29 us -> none  [body(): lax.pmax(peak_all.astype(jnp.bfloat16), 'blk').astype(peak_all.dtype)]
    reduce_scatter x1 -> x0, waiting for transfers between devices: 21.2 us -> none  [body(): numerator = lax.psum_scatter(scaled, 'blk', scatter_dimension=1, tiled=True)]
    dynamic_update_slice x24 -> x0, local copies, waits for them, and re-layouts: 4.38 us -> none  [the longest x8 2.23 us: head_step(): lax.dynamic_update_slice_in_dim(denom_all, partial_den, head_index * grou...]
  transfers between devices with their start and end apart: 3 -> 0, of which waited for: 3 -> 0; matrix products, arithmetic and copies ran while one was open for 0% -> 0% of each run, Pallas kernels for 0% -> 0%
where the time goes in v1:
time: 60.8 us; the launch traced here: 60.2 us
  Pallas kernels  56.1 us (92%)
  other arithmetic  1.45 us (2%)
  local copies, waits for them, and re-layouts  1.38 us (2%)
  between operations  1.31 us (2%)
    pallas_call x1, Pallas kernels, body(): pl.pallas_call(functools.partial(kernel, n, ctx, cols, hpd, chunk), out_s...  56.1 us
    unnamed x1, other arithmetic  1.45 us
    unnamed x1, local copies, waits for them, and re-layouts  1.38 us

profile of v1, /device:TPU:1, one launch (start us, length us, event | category | flops | bytes accessed | tf_op | source)
XLA Modules:
  0.0 60.2 jit_solution(4227628659726215891)
XLA Ops:
  1.3 1.5 %reduce = bf16[8192]{0:T(1024)(128)(2,1)} reduce(bf16[1,8192]{1,0:T(2,128)(2,1)} %param.11, bf16[]{:T(256)} %constant.4), dimensions={0}, to_apply=%param.11.reduce_sub_computation | reduce | bytes 32770 | tf_op args[0]
  2.8 56.1 %shard_map.109 = f32[64,128]{1,0:T(8,128)} custom-call(s32[1]{0:T(128)S(6)} %copy.13.len_ref, s32[1]{0:T(128)S(6)} %copy.14.start_ref, bf16[64,128]{1,0:T(8,128)(2,1)} %bitcast.5, f32[64,128]{1,0:T(8,128)} %bitcast.6, f32[64,128]{1,0:T(8,128)} %bitcast.7, bf16[256,1024]{1,0:T(8,128)(2,1)} %k_hbm.1, bf16[256,1024]{1,0:T(8,128)(2,1)} %v_hbm.1, ...), custom_call_target="tpu_custom_call" | custom-call | tf_op jit(solution)/shard_map/pallas_call | solution.py:240
  58.8 1.4 %copy.15 = f32[1,8192]{1,0:T(1,128)} copy(f32[1,8192]{1,0:T(1,128)} %bitcast.4) | data formatting | bytes 65536
